TPU v7x, 32 devices: a whole 2x2x4 slice. The times are simulated.
32 devices in a mesh: group: 2 (over y), row: 2 (over core), col: 8 (over z, x).
Axes of the slice: x: 2, y: 2, z: 4, core: 2. Of those that a mesh axis runs over, the one named last changes fastest.
Arguments:
- queries: bfloat16 [32, 256, 576], P(('group', 'col')), parts along dimension 0, may hold values from -64 to 64
- prefix_kv: bfloat16 [8192, 576], P(('group', 'row', 'col')), parts along dimension 0, may hold values from -7 to 7
- suffix_kv: bfloat16 [32, 2048, 576], P(('group', 'col'), 'row'), parts along dimension 0, may hold values from -6 to 6
- lengths: int32 [32], P(('group', 'col')), parts along dimension 0, may hold values from 2 to 2048, as said below
Outputs:
- attended: bfloat16 [32, 256, 512], P(('group', 'col')), parts along dimension 0
There are 2 independent parts, one for each index of `group`. A program takes and returns all parts, laid end to end along the dimension named above; each array names one. Nothing has to cross between parts.
Inputs may be any that keep to these rules, and one draw needn't show every extreme that they name: lengths count a request's 2 new tokens, which are its last used slots; some request has exactly 2048.
All inputs are finite; a program needn't handle non-finite values.
Results may differ from a plain program's by a relative error of at most 0.0065.
Values may be sent and summed in bfloat16 or wider, within the bound.
A program may use at most 128 MiB of HBM per device.

v0:
```python
import math

import jax
import jax.numpy as jnp
from jax import lax
from jax.sharding import PartitionSpec as P

H = 128
KVR = 512
POS = 2


softmax_scale = 192.0 ** (-0.5)
floor_value = -1e30


def merged(value, axis, join):
    pieces = jax.tree.map(lambda part: lax.all_gather(part, axis), value)
    head = jax.tree.map(lambda part: part[0], pieces)
    tail = jax.tree.map(lambda part: part[1:], pieces)
    subtotal, _ = lax.scan(lambda subtotal, share: (join(subtotal, share), None), head, tail)
    return subtotal


def absorb(running, query_flat, key_block):
    maximum, weight_sum, blended = running
    scores = (
        jnp.einsum("ml,kl->mk", query_flat, key_block, preferred_element_type=jnp.float32)
        * softmax_scale
    )
    new_max = jnp.maximum(maximum, jnp.max(scores, axis=1))
    weights = jnp.exp(scores - new_max[:, None])
    rescale = jnp.exp(maximum - new_max)
    weight_sum = weight_sum * rescale + jnp.sum(weights, axis=1)
    blended = blended * rescale[:, None] + jnp.dot(
        weights.astype(jnp.bfloat16), key_block[:, :KVR], preferred_element_type=jnp.float32
    )
    return (new_max, weight_sum, blended)


def sweeper(query_flat, running, key_piece):
    key_count = key_piece.shape[0]
    block_size = math.gcd(key_count, 512)
    pieces = key_piece.reshape(key_count // block_size, block_size, key_piece.shape[1])

    def scan_step(carried, key_block):
        return (absorb(carried, query_flat, key_block), None)

    return lax.scan(scan_step, running, pieces)[0]


def suffix_state(queries_own, suffix, lengths, first_key):
    scores = (
        jnp.einsum("rql,rkl->rqk", queries_own, suffix, preferred_element_type=jnp.float32)
        * softmax_scale
    )
    key_index = first_key + jnp.arange(suffix.shape[1], dtype=jnp.int32)
    position = jnp.arange(queries_own.shape[1], dtype=jnp.int32) // H
    key_limit = lengths[:, None] - POS + 1 + position[None, :]
    visible = key_index[None, None, :] < key_limit[:, :, None]
    scores = jnp.where(visible, scores, floor_value)
    maximum = jnp.max(scores, axis=2)
    weights = jnp.where(visible, jnp.exp(scores - maximum[:, :, None]), 0.0)
    weight_sum = jnp.sum(weights, axis=2)
    blended = jnp.einsum(
        "rqk,rkv->rqv",
        weights.astype(jnp.bfloat16),
        suffix[:, :, :KVR],
        preferred_element_type=jnp.float32,
    )
    flat_rows = queries_own.shape[0] * queries_own.shape[1]
    return (
        maximum.reshape(flat_rows),
        weight_sum.reshape(flat_rows),
        blended.reshape(flat_rows, KVR),
    )


def combine(first, second):
    maximum = jnp.maximum(first[0], second[0])
    scale_first = jnp.exp(first[0] - maximum)
    scale_second = jnp.exp(second[0] - maximum)
    weight_sum = first[1] * scale_first + second[1] * scale_second
    blended = first[2] * scale_first[:, None] + second[2] * scale_second[:, None]
    return (maximum, weight_sum, blended)


def per_device(queries, prefix_kv, suffix_kv, lengths):
    request_count, query_rows, latent_width = queries.shape
    first_key = lax.axis_index("row") * suffix_kv.shape[1]
    softmax_state = suffix_state(queries, suffix_kv, lengths, first_key)
    query_flat = queries.reshape(request_count * query_rows, latent_width)
    softmax_state = sweeper(
        query_flat, softmax_state, lax.all_gather(prefix_kv, "col", axis=0, tiled=True)
    )
    maximum, weight_sum, blended = merged(softmax_state, "row", combine)
    return (
        (blended / weight_sum[:, None]).astype(jnp.bfloat16).reshape(request_count, query_rows, KVR)
    )


def solution(mesh):
    return jax.shard_map(
        per_device,
        mesh=mesh,
        in_specs=(
            P(("group", "col"), None, None),
            P(("group", "row", "col"), None),
            P(("group", "col"), "row", None),
            P(("group", "col")),
        ),
        out_specs=P(("group", "col"), None, None),
        check_vma=False,
    )
```

profile of v0, /device:TPU:0, one launch (start us, length us, event | category | flops | bytes accessed | tf_op | source)
XLA Modules:
  0.0 100.4 jit_solution(17647831923459991885)
XLA Ops:
  6.5 0.0 all-gather.8.cloned.1.call-start
  6.5 0.7 all-gather.8.cloned.1.call-update
  7.3 0.0 all-gather.10.cloned.1.call-start
  7.3 1.4 %copy.10 = bf16[2,256,576]{2,1,0:T(8,128)(2,1)S(1)} copy(bf16[2,256,576]{1,2,0:T(8,128)(2,1)} %param.6) | data formatting | bytes 1179648 | tf_op args[0]
  8.7 0.7 broadcast_add_fusion.1
  9.4 0.1 broadcast_add_fusion
  9.4 0.0 copy-start.1
  9.4 3.2 %fusion.7 = (f32[2,256]{1,0:T(2,128)S(1)}, f32[2,256,1024]{2,1,0:T(8,128)S(1)}) fusion(s32[2,256]{1,0:T(2,128)S(1)} %broadcast_add_fusion, s32[1024]{0:T(1024)S(1)} %iota_add_fusion, bf16[2,256,576]{1,2,0:T(8,128)(2,1)} %param.6, bf16[2,1024,576]{1,2,0:T(8,128)(2,1)} %param.8), kind=kOutput, calls=%fused_computation.14 | convolution fusion | flops 606076416 | bytes 5054464 | tf_op jit(solution)/shard_map/rql,rkl->rqk/dot_general | solution.py:54
  12.6 0.7 fusion.9
  13.3 0.0 copy-done.1
  13.3 0.8 fusion.5
  14.2 51.7 %all-gather.8.cloned.1.call-done = bf16[2048,576]{0,1:T(8,128)(2,1)} async-done(((bf16[256,576]{0,1:T(8,128)(2,1)}), bf16[2048,576]{0,1:T(8,128)(2,1)}) %all-gather.8.cloned.1.call-update) | async-done | bytes 2359312 | tf_op jit(solution)/shard_map/all_gather | solution.py:94
  65.9 4.3 %copy.9 = bf16[2048,576]{1,0:T(8,128)(2,1)} copy(bf16[2048,576]{0,1:T(8,128)(2,1)} %all-gather.8.cloned.1.call-done) | data formatting | bytes 4718592 | tf_op jit(solution)/shard_map/all_gather | solution.py:94
  70.2 10.6 %while.2 = (s32[]{:T(128)}, f32[512]{0:T(512)S(1)}, f32[512]{0:T(512)S(1)}, f32[512,512]{1,0:T(8,128)S(1)}, bf16[4,512,576]{2,1,0:T(8,128)(2,1)}, /*index=5*/bf16[512,576]{1,0:T(8,128)(2,1)S(1)}, s32[]{:T(128)}) while((s32[]{:T(128)}, f32[512]{0:T(512)S(1)}, f32[512]{0:T(512)S(1)}, f32[512,512]{1,0:T(8,128)S(1)}, ...), condition=%wide.region_5.6_spmd, body=%wide.region_2.5_spmd.sunk | while | flops 572523520 | bytes 8159321 | solution.py:49
  70.2 1.1 %dynamic-slice_bitcast_fusion.2 = bf16[512,576]{1,0:T(8,128)(2,1)S(1)} fusion(bf16[4,512,576]{2,1,0:T(8,128)(2,1)} %get-tuple-element.155, s32[]{:T(128)S(6)} %copy.18), kind=kLoop, calls=%fused_computation.5.clone.1 | loop fusion | bytes 1179652 | tf_op jit(solution)/shard_map/while/body/jit(dynamic_index_in_dim)/squeeze | solution.py:49
  71.4 0.6 fusion.40
  72.0 0.2 fusion.41
  72.2 0.6 convolution_add_fusion.2
  72.9 1.1 %dynamic-slice_bitcast_fusion.2 = bf16[512,576]{1,0:T(8,128)(2,1)S(1)} fusion(bf16[4,512,576]{2,1,0:T(8,128)(2,1)} %get-tuple-element.155, s32[]{:T(128)S(6)} %copy.18), kind=kLoop, calls=%fused_computation.5.clone.1 | loop fusion | bytes 1179652 | tf_op jit(solution)/shard_map/while/body/jit(dynamic_index_in_dim)/squeeze | solution.py:49
  74.0 0.6 fusion.40
  74.7 0.2 fusion.41
  74.9 0.6 convolution_add_fusion.2
  75.5 1.1 %dynamic-slice_bitcast_fusion.2 = bf16[512,576]{1,0:T(8,128)(2,1)S(1)} fusion(bf16[4,512,576]{2,1,0:T(8,128)(2,1)} %get-tuple-element.155, s32[]{:T(128)S(6)} %copy.18), kind=kLoop, calls=%fused_computation.5.clone.1 | loop fusion | bytes 1179652 | tf_op jit(solution)/shard_map/while/body/jit(dynamic_index_in_dim)/squeeze | solution.py:49
  76.7 0.6 fusion.40
  77.3 0.2 fusion.41
  77.5 0.6 convolution_add_fusion.2
  78.2 1.1 %dynamic-slice_bitcast_fusion.2 = bf16[512,576]{1,0:T(8,128)(2,1)S(1)} fusion(bf16[4,512,576]{2,1,0:T(8,128)(2,1)} %get-tuple-element.155, s32[]{:T(128)S(6)} %copy.18), kind=kLoop, calls=%fused_computation.5.clone.1 | loop fusion | bytes 1179652 | tf_op jit(solution)/shard_map/while/body/jit(dynamic_index_in_dim)/squeeze | solution.py:49
  79.3 0.6 fusion.40
  80.0 0.2 fusion.41
  80.2 0.6 convolution_add_fusion.2
  80.8 0.0 copy-start
  80.9 1.0 copy-done
  81.8 0.0 all-gather.10.cloned.1.call-update
  81.9 1.8 %all-gather.3 = f32[2,1,512]{2,1,0:T(1,128)S(1)} all-gather(f32[1,1,512]{2,1,0:T(1,128)S(1)} %bitcast.29), channel_id=3, replica_groups=mesh['group'=2,'row'=2,'col'=8] {'row'}, dimensions={0}, use_global_device_ids=true | all-gather | bytes 6144 | tf_op jit(solution)/shard_map/all_gather | solution.py:18
  83.6 1.8 %all-gather.4 = f32[2,1,512]{2,1,0:T(1,128)S(1)} all-gather(f32[1,1,512]{2,1,0:T(1,128)S(1)} %bitcast.31), channel_id=4, replica_groups=mesh['group'=2,'row'=2,'col'=8] {'row'}, dimensions={0}, use_global_device_ids=true | all-gather | bytes 6144 | tf_op jit(solution)/shard_map/all_gather | solution.py:18
  85.5 5.3 %all-gather.10.cloned.1.call-done = f32[1024,512]{1,0:T(8,128)} async-done(((f32[512,512]{1,0:T(8,128)}), f32[1024,512]{1,0:T(8,128)}) %all-gather.10.cloned.1.call-update) | async-done | bytes 2097168 | tf_op jit(solution)/shard_map/all_gather | solution.py:18
  90.8 1.7 %fusion.25 = (f32[512,512]{1,0:T(8,128)S(1)}, f32[512,512]{1,0:T(8,128)S(1)}) fusion(f32[1024,512]{1,0:T(8,128)} %all-gather.10.cloned.1.call-done), kind=kLoop, calls=%fused_computation.44 | loop fusion | bytes 4194304 | tf_op jit(solution)/shard_map/slice | solution.py:19
  92.5 1.1 %divide_convert_fusion = bf16[2,256,512]{2,1,0:T(8,128)(2,1)} fusion(f32[2,256,512]{2,1,0:T(8,128)S(1)} %bitcast.27, f32[2,256,512]{2,1,0:T(8,128)S(1)} %bitcast.26, f32[2,256]{1,0:T(2,128)S(1)} %get-tuple-element.81, f32[2,256]{1,0:T(2,128)S(1)} %get-tuple-element.83, f32[2,256]{1,0:T(2,128)S(1)} %get-tuple-element.82), kind=kLoop, calls=%fused_computation.17 | loop fusion | flops 1310720 | bytes 2627584 | tf_op jit(solution)/shard_map/convert_element_type | solution.py:98
  (22 shorter events, 0.2 us)
Async XLA Ops:
  6.5 59.3 %all-gather.8.cloned.1.call-start = ((), (), s32[]{:S(2)}) async-start(), calls=%async_computation | async-start | bytes 2654208 | tf_op jit(solution)/shard_map/all_gather | solution.py:94
  7.3 83.5 %all-gather.10.cloned.1.call-start = ((), (), s32[]{:S(2)}) async-start(), calls=%async_computation.1 | async-start | bytes 3145728 | tf_op jit(solution)/shard_map/all_gather | solution.py:18
  9.4 3.9 %copy-start.1 = (bf16[2,1024,576]{1,2,0:T(8,128)(2,1)S(1)}, bf16[2,1024,576]{1,2,0:T(8,128)(2,1)}, u32[]{:S(2)}) copy-start(bf16[2,1024,576]{1,2,0:T(8,128)(2,1)} %param.8) | copy-start | bytes 7077892
  80.8 1.0 copy-start
Sparse Core Ops, SparseCore 0:
  9.4 56.4 all-gather.7
  82.0 8.7 all-gather.9
where the time goes:
time: 101 us; the launch traced here: 100 us
  waiting for transfers between devices  57.7 us (57%)
  between operations  13.5 us (13%)
  local copies, waits for them, and re-layouts  13.1 us (13%)
  matrix products  8.99 us (9%)
  blocking collectives  3.55 us (4%)
  other arithmetic  3.41 us (3%)
    all_gather x1, waiting for transfers between devices, per_device(): lax.all_gather(prefix_kv, 'col', axis=0, tiled=True)  51.7 us
    all_gather x1, waiting for transfers between devices, merged(): pieces = jax.tree.map(lambda part: lax.all_gather(part, axis), value)  5.27 us
    squeeze x4, local copies, waits for them, and re-layouts, sweeper(): return lax.scan(scan_step, running, pieces)[0]  4.59 us
    all_gather x1, local copies, waits for them, and re-layouts, per_device(): lax.all_gather(prefix_kv, 'col', axis=0, tiled=True)  4.33 us
    all_gather x2, blocking collectives, merged(): pieces = jax.tree.map(lambda part: lax.all_gather(part, axis), value)  3.55 us
    dot_general x1, matrix products, suffix_state(): jnp.einsum('rql,rkl->rqk', queries_own, suffix, preferred_element_type=jn...  3.17 us
    dot_general x4, matrix products, absorb(): jnp.dot(weights.astype(jnp.bfloat16), key_block[:, :KVR], preferred_eleme...  2.5 us
    dot_general x4, matrix products, absorb(): jnp.einsum('ml,kl->mk', query_flat, key_block, preferred_element_type=jnp...  2.5 us
  transfers between devices with their start and end apart: 2, of which 2 were waited for; matrix products, arithmetic and copies ran while one was open for 7% of the time, Pallas kernels for 0%

commit v1 on v0

--- a/solution.py
+++ b/solution.py
@@ -3,6 +3,8 @@
 import jax
 import jax.numpy as jnp
 from jax import lax
+from jax.experimental import pallas as pl
+from jax.experimental.pallas import tpu as pltpu
 from jax.sharding import PartitionSpec as P
 
 H = 128
@@ -99,9 +101,305 @@
     )
 
 
+END_FIRST = [("near", (0, 0, 0)), ("x", (0, 0, 0)), ("near", (0, 0, 1)), ("x", (0, 0, 1))]
+END_EVENTS = [
+    ((0, 1, 0), ["x"]),
+    ((1, 0, 0), []),
+    ((0, 1, 1), []),
+    ((1, 0, 1), ["near"]),
+    ((0, 2, 0), ["x"]),
+    ((1, 1, 0), []),
+    ((0, 2, 1), ["x"]),
+    ((1, 2, 0), []),
+    ((0, 3, 0), ["x"]),
+    ((1, 2, 1), []),
+    ((0, 3, 1), ["x"]),
+    ((1, 3, 0), []),
+    ((1, 1, 1), []),
+    ((1, 3, 1), []),
+]
+MID_FIRST = [
+    ("near", (0, 1, 0)), ("up", (0, 1, 0)), ("x", (0, 1, 1)),
+    ("near", (0, 1, 1)), ("up", (0, 1, 1)), ("x", (0, 1, 0)),
+]
+MID_EVENTS = [
+    ((0, 2, 0), ["near", "x"]),
+    ((0, 0, 0), ["up", "x"]),
+    ((1, 1, 1), []),
+    ((0, 2, 1), ["near"]),
+    ((0, 0, 1), ["up", ("up", (1, 1, 1))]),
+    ((1, 1, 0), []),
+    ((0, 3, 0), ["near", "x"]),
+    ((1, 0, 1), []),
+    ((1, 0, 0), []),
+    ((0, 3, 1), ["near", "x", ("near", (1, 1, 1))]),
+    ((1, 2, 0), []),
+    ((1, 2, 1), []),
+    ((1, 3, 0), []),
+    ((1, 3, 1), []),
+]
+CHUNK = 256
+LOG2E = 1.4426950408889634
+
+
+def dot_t(a, b):
+    return lax.dot_general(a, b, (((1,), (1,)), ((), ())), preferred_element_type=jnp.float32)
+
+
+def gather_attend(
+    q_hbm, prefix_hbm, suffix_hbm, lengths, out_hbm,
+    q, keys, suffix, result, top, total, acc,
+    local_sem, x_send, near_send, up_send, sib_send, recv, sib_recv, suf_send, suf_recv, out_send, out_recv,
+):
+    group, row, col = lax.axis_index("group"), lax.axis_index("row"), lax.axis_index("col")
+    z, x = col // 2, col % 2
+    flip = z // 2
+    place = z + flip * (3 - 2 * z)
+    at_end = place == 0
+    unit = prefix_hbm.shape[0] // 2
+    half_suffix = suffix_hbm.shape[1]
+    other = 1 - row
+
+    def line(p):
+        return p + flip * (3 - 2 * p)
+
+    def index(name):
+        other_x, p, h = name
+        return ((x + other_x - 2 * x * other_x) * 4 + line(p)) * 2 + h
+
+    def slot(u, r):
+        return keys.at[u, pl.ds(pl.multiple_of(r * unit, unit), unit), :]
+
+    devices = {
+        "x": (group, row, z * 2 + 1 - x),
+        "end_near": (group, row, line(1) * 2 + x),
+        "mid_near": (group, row, line(0) * 2 + x),
+        "up": (group, row, line(2) * 2 + x),
+    }
+    sibling = (group, other, col)
+
+    def remote(src, dst, send_sem, recv_sem, device):
+        return pltpu.make_async_remote_copy(
+            src_ref=src, dst_ref=dst, send_sem=send_sem, recv_sem=recv_sem,
+            device_id=device, device_id_type=pl.DeviceIdType.MESH,
+        )
+
+    barrier = pltpu.get_barrier_semaphore()
+
+    def greet(device):
+        pl.semaphore_signal(barrier, inc=1, device_id=device, device_id_type=pl.DeviceIdType.MESH)
+
+    greet(sibling)
+    greet(devices["x"])
+
+    q_in = pltpu.make_async_copy(q_hbm.at[row], q, local_sem.at[0])
+    q_in.start()
+    own_in = []
+    for h in range(2):
+        own_in.append(
+            pltpu.make_async_copy(
+                prefix_hbm.at[pl.ds(h * unit, unit), :], slot(index_own(col, h, z, x), row), local_sem.at[1 + h]
+            )
+        )
+        own_in[-1].start()
+    suffix_in = pltpu.make_async_copy(
+        suffix_hbm.at[row],
+        suffix.at[pl.ds(pl.multiple_of(row * half_suffix, half_suffix), half_suffix), :],
+        local_sem.at[3],
+    )
+    suffix_in.start()
+
+    @pl.when(at_end)
+    def _():
+        greet(devices["end_near"])
+        pl.semaphore_wait(barrier, 3)
+
+    @pl.when(jnp.logical_not(at_end))
+    def _():
+        greet(devices["mid_near"])
+        greet(devices["up"])
+        pl.semaphore_wait(barrier, 4)
+
+    sems = {"x": x_send, "near": near_send, "up": up_send}
+
+    def make_send(kind, counts, link, name, from_hbm):
+        at = counts[link]
+        counts[link] += 1
+        where = (kind + "_near") if link == "near" else link
+
+        def build():
+            u = index(name)
+            src = prefix_hbm.at[pl.ds(name[2] * unit, unit), :] if from_hbm else slot(u, row)
+            return remote(src, slot(u, row), sems[link].at[at], recv.at[u], devices[where])
+
+        return build
+
+    def plan(kind, first, events):
+        counts = {"x": 0, "near": 0, "up": 0}
+        opening = [make_send(kind, counts, link, name, True) for link, name in first]
+        after = []
+        for name, links in events:
+            sends = []
+            for link in links:
+                if isinstance(link, tuple):
+                    sends.append(make_send(kind, counts, link[0], link[1], False))
+                else:
+                    sends.append(make_send(kind, counts, link, name, False))
+            after.append(sends)
+        return opening, after
+
+    end_opening, end_after = plan("end", END_FIRST, END_EVENTS)
+    mid_opening, mid_after = plan("mid", MID_FIRST, MID_EVENTS)
+
+    def both(end_list, mid_list, act):
+        if end_list:
+            @pl.when(at_end)
+            def _():
+                for build in end_list:
+                    act(build())
+        if mid_list:
+            @pl.when(jnp.logical_not(at_end))
+            def _():
+                for build in mid_list:
+                    act(build())
+
+    both(end_opening, mid_opening, lambda copy: copy.start())
+
+    sib_sends = []
+    own_units = [index_own(col, h, z, x) for h in range(2)]
+    for h in range(2):
+        copy = remote(
+            prefix_hbm.at[pl.ds(h * unit, unit), :], slot(own_units[h], row),
+            sib_send.at[h], sib_recv.at[own_units[h]], sibling,
+        )
+        copy.start()
+        sib_sends.append(copy)
+    suffix_half = suffix.at[pl.ds(pl.multiple_of(row * half_suffix, half_suffix), half_suffix), :]
+    suffix_out = remote(suffix_hbm.at[other], suffix_half, suf_send, suf_recv, sibling)
+    suffix_out.start()
+
+    scale = softmax_scale * LOG2E
+    top[...] = jnp.full(top.shape, floor_value, jnp.float32)
+    total[...] = jnp.zeros(total.shape, jnp.float32)
+    acc[...] = jnp.zeros(acc.shape, jnp.float32)
+    length = lengths[row]
+
+    def attend(block, first_key=None):
+        scores = dot_t(q[...], block) * scale
+        if first_key is not None:
+            shape = scores.shape
+            key = first_key + lax.broadcasted_iota(jnp.int32, shape, 1)
+            position = lax.broadcasted_iota(jnp.int32, shape, 0) // H
+            scores = jnp.where(key < length - POS + 1 + position, scores, floor_value)
+        before = top[...]
+        now = jnp.maximum(before, jnp.max(scores, axis=1, keepdims=True))
+        weights = jnp.exp2(scores - now)
+        rescale = jnp.exp2(before - now)
+        top[...] = now
+        total[...] = total[...] * rescale + jnp.sum(weights, axis=1, keepdims=True)
+        acc[...] = acc[...] * rescale + jnp.dot(
+            weights.astype(jnp.bfloat16), block[:, :KVR], preferred_element_type=jnp.float32
+        )
+
+    def await_sibling(u):
+        remote(slot(u, row), slot(u, other), sib_send.at[0], sib_recv.at[u], sibling).wait_recv()
+
+    pieces = half_suffix // CHUNK
+
+    def attend_suffix(i):
+        if i == 0:
+            suffix_in.wait()
+        if i == pieces:
+            remote(
+                suffix_half,
+                suffix.at[pl.ds(pl.multiple_of(other * half_suffix, half_suffix), half_suffix), :],
+                suf_send, suf_recv, sibling,
+            ).wait_recv()
+        part = row if i < pieces else other
+        start = pl.multiple_of(part * half_suffix + (i % pieces) * CHUNK, CHUNK)
+        attend(suffix[pl.ds(start, CHUNK), :], start)
+
+    q_in.wait()
+    for h in range(2):
+        own_in[h].wait()
+    for u in own_units:
+        await_sibling(u)
+        attend(keys[u])
+
+    steps = len(END_EVENTS)
+    names = []
+    for k in range(steps):
+        u = jnp.where(at_end, index(END_EVENTS[k][0]), index(MID_EVENTS[k][0]))
+        remote(slot(u, row), slot(u, row), sib_send.at[0], recv.at[u], sibling).wait_recv()
+        both(end_after[k], mid_after[k], lambda copy: copy.start())
+        copy = remote(slot(u, row), slot(u, row), sib_send.at[2 + k], sib_recv.at[u], sibling)
+        copy.start()
+        sib_sends.append(copy)
+        names.append(u)
+        if k < 2 * pieces:
+            attend_suffix(k)
+        if k >= 1:
+            await_sibling(names[k - 1])
+            attend(keys[names[k - 1]])
+    for i in range(steps, 2 * pieces):
+        attend_suffix(i)
+    await_sibling(names[-1])
+    attend(keys[names[-1]])
+
+    result[...] = (acc[...] / total[...]).astype(jnp.bfloat16)
+    final = remote(result, out_hbm.at[row], out_send, out_recv, sibling)
+    final.start()
+    keep = pltpu.make_async_copy(result, out_hbm.at[row], local_sem.at[4])
+    keep.start()
+    both(
+        end_opening + [b for sends in end_after for b in sends],
+        mid_opening + [b for sends in mid_after for b in sends],
+        lambda copy: copy.wait_send(),
+    )
+    for copy in sib_sends:
+        copy.wait_send()
+    suffix_out.wait_send()
+    keep.wait()
+    final.wait_send()
+    remote(result, out_hbm.at[other], out_send, out_recv, sibling).wait_recv()
+
+
+def index_own(col, h, z, x):
+    return (x * 4 + z) * 2 + h
+
+
+def ring_device(queries, prefix_kv, suffix_kv, lengths):
+    requests, query_rows, width = queries.shape
+    block = prefix_kv.shape[0]
+    half_suffix = suffix_kv.shape[1]
+    dma = pltpu.SemaphoreType.DMA
+    anywhere = pl.BlockSpec(memory_space=pl.ANY)
+    return pl.pallas_call(
+        gather_attend,
+        out_shape=jax.ShapeDtypeStruct((requests, query_rows, KVR), jnp.bfloat16),
+        in_specs=[anywhere, anywhere, anywhere, pl.BlockSpec(memory_space=pltpu.SMEM)],
+        out_specs=anywhere,
+        scratch_shapes=[
+            pltpu.VMEM((query_rows, width), jnp.bfloat16),
+            pltpu.VMEM((16, block, width), jnp.bfloat16),
+            pltpu.VMEM((2 * half_suffix, width), jnp.bfloat16),
+            pltpu.VMEM((query_rows, KVR), jnp.bfloat16),
+            pltpu.VMEM((query_rows, 1), jnp.float32),
+            pltpu.VMEM((query_rows, 1), jnp.float32),
+            pltpu.VMEM((query_rows, KVR), jnp.float32),
+            dma((5,)), dma((7,)), dma((7,)), dma((5,)), dma((16,)), dma((16,)), dma((16,)),
+            dma, dma, dma, dma,
+        ],
+        compiler_params=pltpu.CompilerParams(
+            collective_id=0, has_side_effects=True, vmem_limit_bytes=48 * 1024 * 1024
+        ),
+    )(queries, prefix_kv, suffix_kv, lengths)
+
+
 def solution(mesh):
+    small = dict(mesh.shape) == {"group": 2, "row": 2, "col": 8}
     return jax.shard_map(
-        per_device,
+        ring_device if small else per_device,
         mesh=mesh,
         in_specs=(
             P(("group", "col"), None, None),

time: 101 us -> 47.3 us (0.47)
  waiting for transfers between devices: 57.7 us -> 0 us
  Pallas kernels: 0 us -> 38.9 us
  between operations: 13.5 us -> 0.05 us
  matrix products: 8.99 us -> 0 us
  local copies, waits for them, and re-layouts: 13.1 us -> 8.08 us
  blocking collectives: 3.55 us -> 0 us
  other arithmetic: 3.41 us -> 0 us
    all_gather x2 -> x0, waiting for transfers between devices: 57 us -> none  [the longest x1 51.7 us: per_device(): lax.all_gather(prefix_kv, 'col', axis=0, tiled=True)]
    pallas_call x0 -> x1, Pallas kernels: none -> 38.9 us  [ring_device(): pl.pallas_call(gather_attend, out_shape=jax.ShapeDtypeStruct((requests, q...]
    dot_general x10 -> x0, matrix products: 8.99 us -> none  [the longest x1 3.17 us: suffix_state(): jnp.einsum('rql,rkl->rqk', queries_own, suffix, preferred_element_type=jn...]
    unnamed x7 -> x8, local copies, waits for them, and re-layouts: 2.35 us -> 8.08 us
    squeeze x8 -> x0, local copies, waits for them, and re-layouts: 4.64 us -> none  [the longest x4 4.59 us: sweeper(): return lax.scan(scan_step, running, pieces)[0]]
    all_gather x1 -> x0, local copies, waits for them, and re-layouts: 4.33 us -> none  [per_device(): lax.all_gather(prefix_kv, 'col', axis=0, tiled=True)]
    all_gather x2 -> x0, blocking collectives: 3.55 us -> none  [merged(): pieces = jax.tree.map(lambda part: lax.all_gather(part, axis), value)]
    slice x2 -> x0, local copies, waits for them, and re-layouts: 1.74 us -> none  [merged(): head = jax.tree.map(lambda part: part[0], pieces)]
  transfers between devices with their start and end apart: 2 -> 0, of which waited for: 2 -> 0; matrix products, arithmetic and copies ran while one was open for 7% -> 0% of each run, Pallas kernels for 0% -> 0%
where the time goes in v1:
time: 47.3 us; the launch traced here: 47 us
  Pallas kernels  38.9 us (82%)
  local copies, waits for them, and re-layouts  8.08 us (17%)
    pallas_call x1, Pallas kernels, ring_device(): pl.pallas_call(gather_attend, out_shape=jax.ShapeDtypeStruct((requests, q...  38.9 us
    unnamed x8, local copies, waits for them, and re-layouts  8.08 us

profile of v1, /device:TPU:0, one launch (start us, length us, event | category | flops | bytes accessed | tf_op | source)
XLA Modules:
  0.0 47.0 jit_solution(15054012553949737035)
XLA Ops:
  0.0 1.9 %copy.6.prefix_hbm = bf16[256,576]{1,0:T(8,128)(2,1)} copy(bf16[256,576]{0,1:T(8,128)(2,1)} %param.5) | data formatting | bytes 589824 | tf_op args[1]
  1.9 1.4 %copy.5.q_hbm = bf16[2,256,576]{2,1,0:T(8,128)(2,1)S(1)} copy(bf16[2,256,576]{1,2,0:T(8,128)(2,1)} %param.4) | data formatting | bytes 1179648 | tf_op args[0]
  3.2 0.0 copy-start.1
  3.2 3.1 %copy.7.suffix_hbm = bf16[2,1024,576]{2,1,0:T(8,128)(2,1)S(1)} copy(bf16[2,1024,576]{1,2,0:T(8,128)(2,1)} %param.6) | data formatting | bytes 4718592 | tf_op args[2]
  6.3 0.0 copy-done.1
  6.3 0.0 copy-start
  6.4 1.0 %copy-done = bf16[256,576]{1,0:T(8,128)(2,1)S(1)} copy-done((bf16[256,576]{1,0:T(8,128)(2,1)S(1)}, bf16[256,576]{1,0:T(8,128)(2,1)}, u32[]{:S(2)}) %copy-start) | copy-done | bytes 294936
  7.3 38.9 %shard_map.46 = bf16[2,256,512]{2,1,0:T(8,128)(2,1)S(1)} custom-call(bf16[2,256,576]{2,1,0:T(8,128)(2,1)S(1)} %copy.5.q_hbm, bf16[256,576]{1,0:T(8,128)(2,1)S(1)} %copy-done, bf16[2,1024,576]{2,1,0:T(8,128)(2,1)S(1)} %copy.7.suffix_hbm, s32[2]{0:T(128)S(1)} %copy-done.1), custom_call_target="tpu_custom_call" | custom-call | tf_op jit(solution)/shard_map/pallas_call | solution.py:377
  46.2 0.8 %copy.9 = bf16[2,256,512]{2,1,0:T(8,128)(2,1)} copy(bf16[2,256,512]{2,1,0:T(8,128)(2,1)S(1)} %shard_map.46) | data formatting | bytes 1048576
Async XLA Ops:
  3.2 3.1 %copy-start.1 = (s32[2]{0:T(128)S(1)}, s32[2]{0:T(128)}, u32[]{:S(2)}) copy-start(s32[2]{0:T(128)} %lengths.1) | copy-start | bytes 28
  6.3 1.0 %copy-start = (bf16[256,576]{1,0:T(8,128)(2,1)S(1)}, bf16[256,576]{1,0:T(8,128)(2,1)}, u32[]{:S(2)}) copy-start(bf16[256,576]{1,0:T(8,128)(2,1)} %copy.6.prefix_hbm) | copy-start | bytes 884740

commit v2 on v1

--- a/solution.py
+++ b/solution.py
@@ -148,7 +148,7 @@
 
 def gather_attend(
     q_hbm, prefix_hbm, suffix_hbm, lengths, out_hbm,
-    q, keys, suffix, result, top, total, acc,
+    q_flipped, q, keys, suffix, result, top, total, acc,
     local_sem, x_send, near_send, up_send, sib_send, recv, sib_recv, suf_send, suf_recv, out_send, out_recv,
 ):
     group, row, col = lax.axis_index("group"), lax.axis_index("row"), lax.axis_index("col")
@@ -156,8 +156,8 @@
     flip = z // 2
     place = z + flip * (3 - 2 * z)
     at_end = place == 0
-    unit = prefix_hbm.shape[0] // 2
-    half_suffix = suffix_hbm.shape[1]
+    unit = prefix_hbm.shape[1] // 2
+    half_suffix = suffix_hbm.shape[2]
     other = 1 - row
 
     def line(p):
@@ -168,7 +168,7 @@
         return ((x + other_x - 2 * x * other_x) * 4 + line(p)) * 2 + h
 
     def slot(u, r):
-        return keys.at[u, pl.ds(pl.multiple_of(r * unit, unit), unit), :]
+        return keys.at[u, r]
 
     devices = {
         "x": (group, row, z * 2 + 1 - x),
@@ -192,21 +192,17 @@
     greet(sibling)
     greet(devices["x"])
 
-    q_in = pltpu.make_async_copy(q_hbm.at[row], q, local_sem.at[0])
+    q_in = pltpu.make_async_copy(q_hbm.at[row], q_flipped, local_sem.at[0])
     q_in.start()
     own_in = []
     for h in range(2):
         own_in.append(
             pltpu.make_async_copy(
-                prefix_hbm.at[pl.ds(h * unit, unit), :], slot(index_own(col, h, z, x), row), local_sem.at[1 + h]
+                prefix_hbm.at[:, pl.ds(h * unit, unit)], slot(index_own(col, h, z, x), row), local_sem.at[1 + h]
             )
         )
         own_in[-1].start()
-    suffix_in = pltpu.make_async_copy(
-        suffix_hbm.at[row],
-        suffix.at[pl.ds(pl.multiple_of(row * half_suffix, half_suffix), half_suffix), :],
-        local_sem.at[3],
-    )
+    suffix_in = pltpu.make_async_copy(suffix_hbm.at[row], suffix.at[row], local_sem.at[3])
     suffix_in.start()
 
     @pl.when(at_end)
@@ -229,7 +225,7 @@
 
         def build():
             u = index(name)
-            src = prefix_hbm.at[pl.ds(name[2] * unit, unit), :] if from_hbm else slot(u, row)
+            src = prefix_hbm.at[:, pl.ds(name[2] * unit, unit)] if from_hbm else slot(u, row)
             return remote(src, slot(u, row), sems[link].at[at], recv.at[u], devices[where])
 
         return build
@@ -269,13 +265,12 @@
     own_units = [index_own(col, h, z, x) for h in range(2)]
     for h in range(2):
         copy = remote(
-            prefix_hbm.at[pl.ds(h * unit, unit), :], slot(own_units[h], row),
+            prefix_hbm.at[:, pl.ds(h * unit, unit)], slot(own_units[h], row),
             sib_send.at[h], sib_recv.at[own_units[h]], sibling,
         )
         copy.start()
         sib_sends.append(copy)
-    suffix_half = suffix.at[pl.ds(pl.multiple_of(row * half_suffix, half_suffix), half_suffix), :]
-    suffix_out = remote(suffix_hbm.at[other], suffix_half, suf_send, suf_recv, sibling)
+    suffix_out = remote(suffix_hbm.at[other], suffix.at[row], suf_send, suf_recv, sibling)
     suffix_out.start()
 
     scale = softmax_scale * LOG2E
@@ -285,7 +280,7 @@
     length = lengths[row]
 
     def attend(block, first_key=None):
-        scores = dot_t(q[...], block) * scale
+        scores = jnp.dot(q[...], block, preferred_element_type=jnp.float32) * scale
         if first_key is not None:
             shape = scores.shape
             key = first_key + lax.broadcasted_iota(jnp.int32, shape, 1)
@@ -297,9 +292,10 @@
         rescale = jnp.exp2(before - now)
         top[...] = now
         total[...] = total[...] * rescale + jnp.sum(weights, axis=1, keepdims=True)
-        acc[...] = acc[...] * rescale + jnp.dot(
-            weights.astype(jnp.bfloat16), block[:, :KVR], preferred_element_type=jnp.float32
-        )
+        acc[...] = acc[...] * rescale + dot_t(weights.astype(jnp.bfloat16), block[:KVR, :])
+
+    def attend_unit(u):
+        attend(jnp.concatenate([keys[u, 0], keys[u, 1]], axis=1))
 
     def await_sibling(u):
         remote(slot(u, row), slot(u, other), sib_send.at[0], sib_recv.at[u], sibling).wait_recv()
@@ -310,21 +306,18 @@
         if i == 0:
             suffix_in.wait()
         if i == pieces:
-            remote(
-                suffix_half,
-                suffix.at[pl.ds(pl.multiple_of(other * half_suffix, half_suffix), half_suffix), :],
-                suf_send, suf_recv, sibling,
-            ).wait_recv()
+            remote(suffix.at[row], suffix.at[other], suf_send, suf_recv, sibling).wait_recv()
         part = row if i < pieces else other
-        start = pl.multiple_of(part * half_suffix + (i % pieces) * CHUNK, CHUNK)
-        attend(suffix[pl.ds(start, CHUNK), :], start)
+        start = (i % pieces) * CHUNK
+        attend(suffix[part, :, start : start + CHUNK], part * half_suffix + start)
 
     q_in.wait()
+    q[...] = q_flipped[...].T
     for h in range(2):
         own_in[h].wait()
     for u in own_units:
         await_sibling(u)
-        attend(keys[u])
+        attend_unit(u)
 
     steps = len(END_EVENTS)
     names = []
@@ -340,11 +333,11 @@
             attend_suffix(k)
         if k >= 1:
             await_sibling(names[k - 1])
-            attend(keys[names[k - 1]])
+            attend_unit(names[k - 1])
     for i in range(steps, 2 * pieces):
         attend_suffix(i)
     await_sibling(names[-1])
-    attend(keys[names[-1]])
+    attend_unit(names[-1])
 
     result[...] = (acc[...] / total[...]).astype(jnp.bfloat16)
     final = remote(result, out_hbm.at[row], out_send, out_recv, sibling)
@@ -370,7 +363,7 @@
 
 def ring_device(queries, prefix_kv, suffix_kv, lengths):
     requests, query_rows, width = queries.shape
-    block = prefix_kv.shape[0]
+    unit = prefix_kv.shape[0] // 2
     half_suffix = suffix_kv.shape[1]
     dma = pltpu.SemaphoreType.DMA
     anywhere = pl.BlockSpec(memory_space=pl.ANY)
@@ -380,9 +373,10 @@
         in_specs=[anywhere, anywhere, anywhere, pl.BlockSpec(memory_space=pltpu.SMEM)],
         out_specs=anywhere,
         scratch_shapes=[
+            pltpu.VMEM((width, query_rows), jnp.bfloat16),
             pltpu.VMEM((query_rows, width), jnp.bfloat16),
-            pltpu.VMEM((16, block, width), jnp.bfloat16),
-            pltpu.VMEM((2 * half_suffix, width), jnp.bfloat16),
+            pltpu.VMEM((16, 2, width, unit), jnp.bfloat16),
+            pltpu.VMEM((2, width, half_suffix), jnp.bfloat16),
             pltpu.VMEM((query_rows, KVR), jnp.bfloat16),
             pltpu.VMEM((query_rows, 1), jnp.float32),
             pltpu.VMEM((query_rows, 1), jnp.float32),
@@ -391,9 +385,9 @@
             dma, dma, dma, dma,
         ],
         compiler_params=pltpu.CompilerParams(
-            collective_id=0, has_side_effects=True, vmem_limit_bytes=48 * 1024 * 1024
+            collective_id=0, has_side_effects=True, vmem_limit_bytes=56 * 1024 * 1024
         ),
-    )(queries, prefix_kv, suffix_kv, lengths)
+    )(jnp.swapaxes(queries, 1, 2), prefix_kv.T, jnp.swapaxes(suffix_kv, 1, 2), lengths)
 
 
 def solution(mesh):

time: 47.3 us -> 39.3 us (0.83)
  local copies, waits for them, and re-layouts: 8.08 us -> 1.87 us
  Pallas kernels: 38.9 us -> 37.3 us
    unnamed x8 -> x1, local copies, waits for them, and re-layouts: 8.08 us -> 1.87 us
    pallas_call x1, Pallas kernels: 38.9 us -> 37.3 us  [ring_device(): pl.pallas_call(gather_attend, out_shape=jax.ShapeDtypeStruct((requests, q...]
where the time goes in v2:
time: 39.3 us; the launch traced here: 39.2 us
  Pallas kernels  37.3 us (95%)
  local copies, waits for them, and re-layouts  1.87 us (5%)
    pallas_call x1, Pallas kernels, ring_device(): pl.pallas_call(gather_attend, out_shape=jax.ShapeDtypeStruct((requests, q...  37.3 us
    unnamed x1, local copies, waits for them, and re-layouts  1.87 us

profile of v2, /device:TPU:0, one launch (start us, length us, event | category | flops | bytes accessed | tf_op | source)
XLA Modules:
  0.0 39.2 jit_solution(13080238201193945098)
XLA Ops:
  0.0 37.3 %shard_map.46 = bf16[2,256,512]{2,1,0:T(8,128)(2,1)} custom-call(bf16[2,576,256]{2,1,0:T(8,128)(2,1)} %bitcast.4, bf16[576,256]{1,0:T(8,128)(2,1)} %bitcast.5, bf16[2,576,1024]{2,1,0:T(8,128)(2,1)} %bitcast.3, s32[2]{0:T(128)} %lengths.1), custom_call_target="tpu_custom_call" | custom-call | tf_op jit(solution)/shard_map/pallas_call | solution.py:370
  37.3 1.9 %copy.6 = bf16[2,256,512]{2,1,0:T(8,128)(2,1)} copy(bf16[2,256,512]{2,1,0:T(8,128)(2,1)} %shard_map.46) | data formatting | bytes 1048576

commit v3 on v2

--- a/solution.py
+++ b/solution.py
@@ -138,8 +138,19 @@
     ((1, 3, 0), []),
     ((1, 3, 1), []),
 ]
+END_GROUPS = [2] * 7
+MID_GROUPS = [3, 3, 3, 2, 2, 1]
+PARTS = 2
 CHUNK = 256
 LOG2E = 1.4426950408889634
+
+
+def in_parts(events, groups):
+    order, start = [], 0
+    for size in groups:
+        order += [(k, part) for part in range(PARTS) for k in range(start, start + size)]
+        start += size
+    return order
 
 
 def dot_t(a, b):
@@ -218,34 +229,45 @@
 
     sems = {"x": x_send, "near": near_send, "up": up_send}
 
-    def make_send(kind, counts, link, name, from_hbm):
+    span = prefix_hbm.shape[0] // PARTS
+
+    def piece(u, r, part):
+        return keys.at[u, r, pl.ds(part * span, span), :]
+
+    def own_piece(h, part):
+        return prefix_hbm.at[pl.ds(part * span, span), pl.ds(h * unit, unit)]
+
+    def make_send(kind, counts, link, name, part, from_hbm):
         at = counts[link]
         counts[link] += 1
         where = (kind + "_near") if link == "near" else link
 
         def build():
             u = index(name)
-            src = prefix_hbm.at[:, pl.ds(name[2] * unit, unit)] if from_hbm else slot(u, row)
-            return remote(src, slot(u, row), sems[link].at[at], recv.at[u], devices[where])
+            src = own_piece(name[2], part) if from_hbm else piece(u, row, part)
+            return remote(src, piece(u, row, part), sems[link].at[at], recv.at[u, part], devices[where])
 
         return build
 
-    def plan(kind, first, events):
+    def plan(kind, first, events, order):
         counts = {"x": 0, "near": 0, "up": 0}
-        opening = [make_send(kind, counts, link, name, True) for link, name in first]
+        opening = [
+            make_send(kind, counts, link, name, part, True)
+            for at in range(0, len(first), len(first) // 2)
+            for part in range(PARTS)
+            for link, name in first[at : at + len(first) // 2]
+        ]
         after = []
-        for name, links in events:
-            sends = []
-            for link in links:
-                if isinstance(link, tuple):
-                    sends.append(make_send(kind, counts, link[0], link[1], False))
-                else:
-                    sends.append(make_send(kind, counts, link, name, False))
-            after.append(sends)
+        for k, part in order:
+            name, links = events[k]
+            pairs = [link if isinstance(link, tuple) else (link, name) for link in links]
+            after.append([make_send(kind, counts, link, sent, part, False) for link, sent in pairs])
         return opening, after
 
-    end_opening, end_after = plan("end", END_FIRST, END_EVENTS)
-    mid_opening, mid_after = plan("mid", MID_FIRST, MID_EVENTS)
+    end_order = in_parts(END_EVENTS, END_GROUPS)
+    mid_order = in_parts(MID_EVENTS, MID_GROUPS)
+    end_opening, end_after = plan("end", END_FIRST, END_EVENTS, end_order)
+    mid_opening, mid_after = plan("mid", MID_FIRST, MID_EVENTS, mid_order)
 
     def both(end_list, mid_list, act):
         if end_list:
@@ -266,7 +288,7 @@
     for h in range(2):
         copy = remote(
             prefix_hbm.at[:, pl.ds(h * unit, unit)], slot(own_units[h], row),
-            sib_send.at[h], sib_recv.at[own_units[h]], sibling,
+            sib_send.at[h, 0], sib_recv.at[own_units[h], 0], sibling,
         )
         copy.start()
         sib_sends.append(copy)
@@ -297,8 +319,15 @@
     def attend_unit(u):
         attend(jnp.concatenate([keys[u, 0], keys[u, 1]], axis=1))
 
-    def await_sibling(u):
-        remote(slot(u, row), slot(u, other), sib_send.at[0], sib_recv.at[u], sibling).wait_recv()
+    def await_sibling(u, whole=False):
+        if whole:
+            remote(slot(u, row), slot(u, other), sib_send.at[0, 0], sib_recv.at[u, 0], sibling).wait_recv()
+        else:
+            for part in range(PARTS):
+                remote(
+                    piece(u, row, part), piece(u, other, part),
+                    sib_send.at[0, part], sib_recv.at[u, part], sibling,
+                ).wait_recv()
 
     pieces = half_suffix // CHUNK
 
@@ -316,28 +345,49 @@
     for h in range(2):
         own_in[h].wait()
     for u in own_units:
-        await_sibling(u)
+        await_sibling(u, True)
         attend_unit(u)
 
-    steps = len(END_EVENTS)
-    names = []
-    for k in range(steps):
-        u = jnp.where(at_end, index(END_EVENTS[k][0]), index(MID_EVENTS[k][0]))
-        remote(slot(u, row), slot(u, row), sib_send.at[0], recv.at[u], sibling).wait_recv()
-        both(end_after[k], mid_after[k], lambda copy: copy.start())
-        copy = remote(slot(u, row), slot(u, row), sib_send.at[2 + k], sib_recv.at[u], sibling)
+    def finished(order):
+        return [k for k, part in order if part == PARTS - 1]
+
+    def ready(order):
+        return [at for at, (k, part) in enumerate(order) if part == PARTS - 1]
+
+    units = [
+        jnp.where(at_end, index(END_EVENTS[a][0]), index(MID_EVENTS[b][0]))
+        for a, b in zip(finished(end_order), finished(mid_order))
+    ]
+    due = [max(a, b) + 1 for a, b in zip(ready(end_order), ready(mid_order))]
+    steps = len(end_order)
+    done, suffix_done = 0, 0
+    for i in range(steps):
+        a, b = end_order[i], mid_order[i]
+        u = jnp.where(at_end, index(END_EVENTS[a[0]][0]), index(MID_EVENTS[b[0]][0]))
+        if a[1] == b[1]:
+            part = a[1]
+        else:
+            part = jnp.where(at_end, a[1], b[1])
+        here = (u, row, pl.ds(pl.multiple_of(part * span, 16), span), slice(None))
+        remote(keys.at[here], keys.at[here], sib_send.at[0, 0], recv.at[u, part], sibling).wait_recv()
+        both(end_after[i], mid_after[i], lambda copy: copy.start())
+        copy = remote(
+            keys.at[here], keys.at[here], sib_send.at[2 + i // PARTS, i % PARTS], sib_recv.at[u, part], sibling
+        )
         copy.start()
         sib_sends.append(copy)
-        names.append(u)
-        if k < 2 * pieces:
-            attend_suffix(k)
-        if k >= 1:
-            await_sibling(names[k - 1])
-            attend_unit(names[k - 1])
-    for i in range(steps, 2 * pieces):
-        attend_suffix(i)
-    await_sibling(names[-1])
-    attend_unit(names[-1])
+        if i % 2 == 0 and suffix_done < 2 * pieces:
+            attend_suffix(suffix_done)
+            suffix_done += 1
+        while done < len(due) and due[done] <= i:
+            await_sibling(units[done])
+            attend_unit(units[done])
+            done += 1
+    for at in range(suffix_done, 2 * pieces):
+        attend_suffix(at)
+    for at in range(done, len(due)):
+        await_sibling(units[at])
+        attend_unit(units[at])
 
     result[...] = (acc[...] / total[...]).astype(jnp.bfloat16)
     final = remote(result, out_hbm.at[row], out_send, out_recv, sibling)
@@ -381,11 +431,12 @@
             pltpu.VMEM((query_rows, 1), jnp.float32),
             pltpu.VMEM((query_rows, 1), jnp.float32),
             pltpu.VMEM((query_rows, KVR), jnp.float32),
-            dma((5,)), dma((7,)), dma((7,)), dma((5,)), dma((16,)), dma((16,)), dma((16,)),
+            dma((5,)), dma((7 * PARTS,)), dma((7 * PARTS,)), dma((5 * PARTS,)),
+            dma((16, PARTS)), dma((16, PARTS)), dma((16, PARTS)),
             dma, dma, dma, dma,
         ],
         compiler_params=pltpu.CompilerParams(
-            collective_id=0, has_side_effects=True, vmem_limit_bytes=56 * 1024 * 1024
+            collective_id=0, has_side_effects=True, vmem_limit_bytes=57344 * 1024
         ),
     )(jnp.swapaxes(queries, 1, 2), prefix_kv.T, jnp.swapaxes(suffix_kv, 1, 2), lengths)
 

time: 39.3 us -> 40.5 us (1.031)
  Pallas kernels: 37.3 us -> 38.4 us
    pallas_call x1, Pallas kernels: 37.3 us -> 38.4 us  [ring_device(): pl.pallas_call(gather_attend, out_shape=jax.ShapeDtypeStruct((requests, q...]
where the time goes in v3:
time: 40.5 us; the launch traced here: 40.3 us
  Pallas kernels  38.4 us (95%)
  local copies, waits for them, and re-layouts  1.87 us (5%)
    pallas_call x1, Pallas kernels, ring_device(): pl.pallas_call(gather_attend, out_shape=jax.ShapeDtypeStruct((requests, q...  38.4 us
    unnamed x1, local copies, waits for them, and re-layouts  1.87 us

profile of v3, /device:TPU:0, one launch (start us, length us, event | category | flops | bytes accessed | tf_op | source)
XLA Modules:
  0.0 40.3 jit_solution(17483965641839646684)
XLA Ops:
  0.0 38.4 %shard_map.46 = bf16[2,256,512]{2,1,0:T(8,128)(2,1)} custom-call(bf16[2,576,256]{2,1,0:T(8,128)(2,1)} %bitcast.4, bf16[576,256]{1,0:T(8,128)(2,1)} %bitcast.5, bf16[2,576,1024]{2,1,0:T(8,128)(2,1)} %bitcast.3, s32[2]{0:T(128)} %lengths.1), custom_call_target="tpu_custom_call" | custom-call | tf_op jit(solution)/shard_map/pallas_call | solution.py:420
  38.5 1.9 %copy.6 = bf16[2,256,512]{2,1,0:T(8,128)(2,1)} copy(bf16[2,256,512]{2,1,0:T(8,128)(2,1)} %shard_map.46) | data formatting | bytes 1048576

commit v4 on v2

--- a/solution.py
+++ b/solution.py
@@ -319,6 +319,8 @@
         await_sibling(u)
         attend_unit(u)
 
+    for i in range(4):
+        attend_suffix(i)
     steps = len(END_EVENTS)
     names = []
     for k in range(steps):
@@ -329,8 +331,8 @@
         copy.start()
         sib_sends.append(copy)
         names.append(u)
-        if k < 2 * pieces:
-            attend_suffix(k)
+        if k >= 4 and k < 12 - 4:
+            attend_suffix(k - 4 + 4)
         if k >= 1:
             await_sibling(names[k - 1])
             attend_unit(names[k - 1])

time: 39.3 us -> 37.7 us (0.959)
  Pallas kernels: 37.3 us -> 35.7 us
    pallas_call x1, Pallas kernels: 37.3 us -> 35.7 us  [ring_device(): pl.pallas_call(gather_attend, out_shape=jax.ShapeDtypeStruct((requests, q...]
where the time goes in v4:
time: 37.7 us; the launch traced here: 37.6 us
  Pallas kernels  35.7 us (95%)
  local copies, waits for them, and re-layouts  1.87 us (5%)
    pallas_call x1, Pallas kernels, ring_device(): pl.pallas_call(gather_attend, out_shape=jax.ShapeDtypeStruct((requests, q...  35.7 us
    unnamed x1, local copies, waits for them, and re-layouts  1.87 us

profile of v4, /device:TPU:0, one launch (start us, length us, event | category | flops | bytes accessed | tf_op | source)
XLA Modules:
  0.0 37.6 jit_solution(14674817400319044982)
XLA Ops:
  0.0 35.7 %shard_map.46 = bf16[2,256,512]{2,1,0:T(8,128)(2,1)} custom-call(bf16[2,576,256]{2,1,0:T(8,128)(2,1)} %bitcast.4, bf16[576,256]{1,0:T(8,128)(2,1)} %bitcast.5, bf16[2,576,1024]{2,1,0:T(8,128)(2,1)} %bitcast.3, s32[2]{0:T(128)} %lengths.1), custom_call_target="tpu_custom_call" | custom-call | tf_op jit(solution)/shard_map/pallas_call | solution.py:372
  35.7 1.9 %copy.6 = bf16[2,256,512]{2,1,0:T(8,128)(2,1)} copy(bf16[2,256,512]{2,1,0:T(8,128)(2,1)} %shard_map.46) | data formatting | bytes 1048576

commit v5 on v4

--- a/solution.py
+++ b/solution.py
@@ -101,22 +101,22 @@
     )
 
 
-END_FIRST = [("near", (0, 0, 0)), ("x", (0, 0, 0)), ("near", (0, 0, 1)), ("x", (0, 0, 1))]
+END_FIRST = [("near", (0, 0, 0)), ("x", (0, 0, 1)), ("near", (0, 0, 1)), ("x", (0, 0, 0))]
 END_EVENTS = [
     ((0, 1, 0), ["x"]),
+    ((1, 0, 1), ["near"]),
+    ((0, 1, 1), ["x"]),
     ((1, 0, 0), []),
-    ((0, 1, 1), []),
-    ((1, 0, 1), ["near"]),
     ((0, 2, 0), ["x"]),
     ((1, 1, 0), []),
     ((0, 2, 1), ["x"]),
+    ((1, 1, 1), []),
+    ((0, 3, 0), ["x"]),
     ((1, 2, 0), []),
-    ((0, 3, 0), ["x"]),
+    ((0, 3, 1), []),
     ((1, 2, 1), []),
-    ((0, 3, 1), ["x"]),
+    ((1, 3, 1), []),
     ((1, 3, 0), []),
-    ((1, 1, 1), []),
-    ((1, 3, 1), []),
 ]
 MID_FIRST = [
     ("near", (0, 1, 0)), ("up", (0, 1, 0)), ("x", (0, 1, 1)),
@@ -127,16 +127,16 @@
     ((0, 0, 0), ["up", "x"]),
     ((1, 1, 1), []),
     ((0, 2, 1), ["near"]),
-    ((0, 0, 1), ["up", ("up", (1, 1, 1))]),
+    ((0, 0, 1), ["up"]),
     ((1, 1, 0), []),
     ((0, 3, 0), ["near", "x"]),
-    ((1, 0, 1), []),
+    ((1, 0, 1), ["up", ("up", (1, 1, 1))]),
     ((1, 0, 0), []),
-    ((0, 3, 1), ["near", "x", ("near", (1, 1, 1))]),
+    ((0, 3, 1), ["near"]),
     ((1, 2, 0), []),
+    ((1, 3, 1), ["near"]),
+    ((1, 3, 0), []),
     ((1, 2, 1), []),
-    ((1, 3, 0), []),
-    ((1, 3, 1), []),
 ]
 CHUNK = 256
 LOG2E = 1.4426950408889634
@@ -383,7 +383,7 @@
             pltpu.VMEM((query_rows, 1), jnp.float32),
             pltpu.VMEM((query_rows, 1), jnp.float32),
             pltpu.VMEM((query_rows, KVR), jnp.float32),
-            dma((5,)), dma((7,)), dma((7,)), dma((5,)), dma((16,)), dma((16,)), dma((16,)),
+            dma((5,)), dma((7,)), dma((7,)), dma((6,)), dma((16,)), dma((16,)), dma((16,)),
             dma, dma, dma, dma,
         ],
         compiler_params=pltpu.CompilerParams(

time: 37.7 us -> 36.3 us (0.963)
  Pallas kernels: 35.7 us -> 34.3 us
    pallas_call x1, Pallas kernels: 35.7 us -> 34.3 us  [ring_device(): pl.pallas_call(gather_attend, out_shape=jax.ShapeDtypeStruct((requests, q...]
where the time goes in v5:
time: 36.3 us; the launch traced here: 36.2 us
  Pallas kernels  34.3 us (94%)
  local copies, waits for them, and re-layouts  1.87 us (5%)
    pallas_call x1, Pallas kernels, ring_device(): pl.pallas_call(gather_attend, out_shape=jax.ShapeDtypeStruct((requests, q...  34.3 us
    unnamed x1, local copies, waits for them, and re-layouts  1.87 us

profile of v5, /device:TPU:0, one launch (start us, length us, event | category | flops | bytes accessed | tf_op | source)
XLA Modules:
  0.0 36.2 jit_solution(1626757121068962853)
XLA Ops:
  0.0 34.3 %shard_map.46 = bf16[2,256,512]{2,1,0:T(8,128)(2,1)} custom-call(bf16[2,576,256]{2,1,0:T(8,128)(2,1)} %bitcast.4, bf16[576,256]{1,0:T(8,128)(2,1)} %bitcast.5, bf16[2,576,1024]{2,1,0:T(8,128)(2,1)} %bitcast.3, s32[2]{0:T(128)} %lengths.1), custom_call_target="tpu_custom_call" | custom-call | tf_op jit(solution)/shard_map/pallas_call | solution.py:372
  34.3 1.9 %copy.6 = bf16[2,256,512]{2,1,0:T(8,128)(2,1)} copy(bf16[2,256,512]{2,1,0:T(8,128)(2,1)} %shard_map.46) | data formatting | bytes 1048576

commit v6 on v5

--- a/solution.py
+++ b/solution.py
@@ -331,8 +331,8 @@
         copy.start()
         sib_sends.append(copy)
         names.append(u)
-        if k >= 4 and k < 12 - 4:
-            attend_suffix(k - 4 + 4)
+        if k >= 8 and k < 12:
+            attend_suffix(k - 4)
         if k >= 1:
             await_sibling(names[k - 1])
             attend_unit(names[k - 1])

time: 36.3 us -> 35.2 us (0.970)
  Pallas kernels: 34.3 us -> 33.1 us
    pallas_call x1, Pallas kernels: 34.3 us -> 33.1 us  [ring_device(): pl.pallas_call(gather_attend, out_shape=jax.ShapeDtypeStruct((requests, q...]
where the time goes in v6:
time: 35.2 us; the launch traced here: 35 us
  Pallas kernels  33.1 us (94%)
  local copies, waits for them, and re-layouts  1.87 us (5%)
    pallas_call x1, Pallas kernels, ring_device(): pl.pallas_call(gather_attend, out_shape=jax.ShapeDtypeStruct((requests, q...  33.1 us
    unnamed x1, local copies, waits for them, and re-layouts  1.87 us

profile of v6, /device:TPU:0, one launch (start us, length us, event | category | flops | bytes accessed | tf_op | source)
XLA Modules:
  0.0 35.0 jit_solution(17356565679783627034)
XLA Ops:
  0.0 33.1 %shard_map.46 = bf16[2,256,512]{2,1,0:T(8,128)(2,1)} custom-call(bf16[2,576,256]{2,1,0:T(8,128)(2,1)} %bitcast.4, bf16[576,256]{1,0:T(8,128)(2,1)} %bitcast.5, bf16[2,576,1024]{2,1,0:T(8,128)(2,1)} %bitcast.3, s32[2]{0:T(128)} %lengths.1), custom_call_target="tpu_custom_call" | custom-call | tf_op jit(solution)/shard_map/pallas_call | solution.py:372
  33.2 1.9 %copy.6 = bf16[2,256,512]{2,1,0:T(8,128)(2,1)} copy(bf16[2,256,512]{2,1,0:T(8,128)(2,1)} %shard_map.46) | data formatting | bytes 1048576
